TPU v7x, 32 devices: a whole 2x2x4 slice. The times are simulated.
32 devices in a mesh: req: 8 (over z, x), tp: 4 (over y, core).
Axes of the slice: x: 2, y: 2, z: 4, core: 2. Of those that a mesh axis runs over, the one named last changes fastest.
Arguments:
- queries: bfloat16 [512, 8192], P('req', 'tp'), may hold values from -5 to 5
- key_cache: bfloat16 [512, 64, 1024], P('req', None, 'tp'), may hold values from -5 to 5
- value_cache: bfloat16 [512, 64, 1024], P('req', None, 'tp'), may hold values from -5 to 5
- lengths: int32 [512], P('req'), may hold values from 8 to 64, as said below
- row_adapter_index: int32 [512], replicated, may hold values from 0 to 255, as said below
- down_weight: bfloat16 [256, 8192, 64], P('req', 'tp'), may hold values from -0.0625 to 0.0625
- up_weight: bfloat16 [256, 64, 8192], P('req', None, 'tp'), may hold values from -1.5 to 1.5
Outputs:
- attn_out: bfloat16 [512, 8192], P('req', 'tp')
- adapter_output: bfloat16 [512, 8192], P('req', 'tp')
Inputs may be any that keep to these rules, and one draw needn't show every extreme that they name: `row_adapter_index`: adapter a belongs to owner a // 32, the index of req that holds it. Among the 64 rows of one index of req (aligned blocks of the row dimension), at most 8 name adapters of one owner; some owner receives exactly 8 rows from every block. `lengths`: every index of req holds a row of length 64.
All inputs are finite; a program needn't handle non-finite values.
Results may differ from a plain program's by a relative error of at most 0.019.
Values may be sent and summed in bfloat16 or wider, within the bound.
A program may use at most 64 MiB of HBM per device.

v0:
```python
import jax
import jax.numpy as jnp
from jax import lax
from jax.sharding import PartitionSpec as P

HEAD_DIM = 128
CAP = 8
ROWS_PER_INDEX = 64
CTX = 64
ADP_REQ = 32
GROUP = 8


def attend(queries, key_cache, value_cache, lengths):
    count = queries.shape[0]
    kv_local = key_cache.shape[2] // HEAD_DIM
    query_heads = queries.reshape(count, kv_local, GROUP, HEAD_DIM)
    key_heads = key_cache.reshape(count, CTX, kv_local, HEAD_DIM)
    value_heads = value_cache.reshape(count, CTX, kv_local, HEAD_DIM)
    scores = jnp.einsum(
        "rkgd,rckd->rkgc", query_heads, key_heads, preferred_element_type=jnp.float32
    ) * HEAD_DIM ** (-0.5)
    valid = jnp.arange(CTX)[None, :] < lengths[:, None]
    scores = jnp.where(valid[:, None, None, :], scores, -jnp.inf)
    highest = jnp.max(scores, axis=3, keepdims=True)
    expo = jnp.exp(scores - highest)
    weights = (expo / jnp.sum(expo, axis=3, keepdims=True)).astype(jnp.bfloat16)
    mixed = jnp.einsum("rkgc,rckd->rkgd", weights, value_heads, preferred_element_type=jnp.float32)
    return mixed.astype(jnp.bfloat16).reshape(count, kv_local * GROUP * HEAD_DIM)


def apply_adapter(incoming_slots, adapter_of_slot, down_weight, up_weight):
    adapter_grouped = jnp.einsum(
        "pv,hvo->pho", incoming_slots, down_weight, preferred_element_type=jnp.float32
    )
    partial_shrink = jnp.einsum("sar,sa->sr", adapter_grouped, adapter_of_slot)
    shrink = lax.psum(partial_shrink, "tp").astype(jnp.bfloat16)
    spread_rows = shrink[:, None, :] * adapter_of_slot.astype(jnp.bfloat16)[:, :, None]
    return jnp.einsum(
        "fmb,mbc->fc", spread_rows, up_weight, preferred_element_type=jnp.float32
    ).astype(jnp.bfloat16)


def on_device(queries, key_cache, value_cache, lengths, row_adapter_index, down_weight, up_weight):
    decode_attention = attend(queries, key_cache, value_cache, lengths)
    n_req = lax.axis_size("req")
    my_index = lax.axis_index("req")
    slot_total = n_req * CAP
    all_rows = n_req * ROWS_PER_INDEX
    block_list = row_adapter_index.reshape(n_req, ROWS_PER_INDEX)
    owners = block_list // ADP_REQ
    order = jnp.arange(ROWS_PER_INDEX)
    earlier = order[None, :] < order[:, None]
    same_owner = owners[:, :, None] == owners[:, None, :]
    ranks = jnp.sum(jnp.logical_and(same_owner, earlier[None, :, :]), axis=2)
    recv_slot = jnp.where(owners == my_index, jnp.arange(n_req)[:, None] * CAP + ranks, -1).reshape(
        all_rows
    )
    recv_onehot = (jnp.arange(slot_total)[:, None] == recv_slot[None, :]).astype(jnp.bfloat16)
    local_adapter = row_adapter_index % ADP_REQ
    adapter_onehot = (local_adapter[:, None] == jnp.arange(ADP_REQ)[None, :]).astype(jnp.bfloat16)
    adapter_of_slot = jnp.dot(recv_onehot, adapter_onehot, preferred_element_type=jnp.float32)
    picker = recv_onehot
    gathered_rows = jnp.dot(
        picker,
        lax.all_gather(decode_attention, "req", axis=0, tiled=True),
        preferred_element_type=jnp.float32,
    ).astype(jnp.bfloat16)
    adapter_delta = apply_adapter(gathered_rows, adapter_of_slot, down_weight, up_weight)
    picker = recv_onehot
    adapter_output = lax.psum_scatter(
        lax.dot_general(
            picker, adapter_delta, (((0,), (0,)), ((), ())), preferred_element_type=jnp.float32
        ).astype(jnp.bfloat16),
        "req",
        scatter_dimension=0,
        tiled=True,
    )
    return (decode_attention, adapter_output)


def solution(mesh):
    in_specs = (
        P("req", "tp"),
        P("req", None, "tp"),
        P("req", None, "tp"),
        P("req"),
        P(),
        P("req", "tp", None),
        P("req", None, "tp"),
    )
    out_specs = (P("req", "tp"), P("req", "tp"))
    return jax.shard_map(
        on_device, mesh=mesh, in_specs=in_specs, out_specs=out_specs, check_vma=False
    )
```

profile of v0, /device:TPU:0, one launch (start us, length us, event | category | flops | bytes accessed | tf_op | source)
XLA Modules:
  0.0 166.1 jit_solution(13617282307648895008)
XLA Ops:
  7.2 0.0 copy-start
  7.2 0.0 all-gather.2.cloned.1.call-start
  7.2 1.1 copy.21
  8.4 0.7 iota_compare_fusion.8
  9.1 3.0 %fusion.37 = (f32[64,2,8]{2,1,0:T(2,128)S(1)}, f32[64,2,8,64]{3,2,1,0:T(8,128)S(1)}) fusion(bf16[64,2,8,128]{3,2,1,0:T(8,128)(2,1)S(1)} %bitcast.52, pred[64,64]{1,0:T(8,128)(4,1)S(1)} %iota_compare_fusion.8, bf16[64,64,256]{2,1,0:T(8,128)(2,1)} %param.8), kind=kOutput, calls=%fused_computation.54 | convolution fusion | flops 17039424 | bytes 2629632 | tf_op jit(solution)/shard_map/sub | solution.py:26
  12.1 0.0 copy-done
  12.1 0.0 copy-start.1
  12.1 0.7 fusion.17
  12.8 0.8 copy.45
  13.6 0.0 all-gather.2.cloned.1.call-update
  13.6 0.0 reduce-scatter.2.cloned.1.call-start
  13.7 0.0 copy-done.1
  13.7 0.1 reshape.145
  13.8 0.3 convert_reduce_fusion
  14.1 0.1 broadcast_add_fusion
  14.2 0.1 add.36
  14.3 0.3 fusion.26
  14.6 0.1 copy.14
  14.7 0.1 copy.16
  14.8 50.9 %all-gather.2.cloned.1.call-done = bf16[512,2048]{1,0:T(8,128)(2,1)} async-done(((bf16[64,2048]{1,0:T(8,128)(2,1)}), bf16[512,2048]{1,0:T(8,128)(2,1)}) %all-gather.2.cloned.1.call-update) | async-done | bytes 2097168 | tf_op jit(solution)/shard_map/all_gather | solution.py:66
  65.8 8.5 %fusion.22 = bf16[64,32,64]{2,0,1:T(8,128)(2,1)S(1)} fusion(bf16[32,2048,64]{1,2,0:T(8,128)(2,1)} %param.12, bf16[512,2048]{1,0:T(8,128)(2,1)} %all-gather.2.cloned.1.call-done, s32[512]{0:T(512)S(1)} %get-tuple-element.2), kind=kOutput, calls=%fused_computation.19 | convolution fusion | flops 671252480 | bytes 10749952 | tf_op jit(solution)/shard_map/pv,hvo->pho/dot_general | solution.py:33
  74.3 0.4 fusion.20
  74.7 10.3 %psum.7 = bf16[64,64]{1,0:T(8,128)(2,1)S(1)} all-reduce(f32[64,64]{1,0:T(8,128)S(1)} %bitcast.55), channel_id=1, replica_groups=mesh['req'=8,'tp'=4] {'tp'}, use_global_device_ids=true, to_apply=%region_3.4 | all-reduce | flops 4096 | bytes 24576 | tf_op jit(solution)/shard_map/psum | solution.py:37
  85.0 0.3 broadcast_multiply_fusion
  85.3 7.0 %convolution_convert_fusion = bf16[512,2048]{1,0:T(8,128)(2,1)} fusion(bf16[32,64,2048]{2,1,0:T(8,128)(2,1)} %param.13, bf16[64,32,64]{2,1,0:T(8,128)(2,1)S(1)} %broadcast_multiply_fusion, s32[512]{0:T(512)S(1)} %get-tuple-element.2), kind=kOutput, calls=%fused_computation.1 | convolution fusion | flops 672301056 | bytes 10749952 | tf_op jit(solution)/shard_map/dot_general | solution.py:72
  92.4 0.0 reduce-scatter.2.cloned.1.call-update
  92.4 66.9 %reduce-scatter.2.cloned.1.call-done = bf16[64,2048]{1,0:T(8,128)(2,1)} async-done(((bf16[512,2048]{1,0:T(8,128)(2,1)}), bf16[64,2048]{1,0:T(8,128)(2,1)}) %reduce-scatter.2.cloned.1.call-update) | async-done | bytes 262160 | tf_op jit(solution)/shard_map/reduce_scatter | solution.py:71
  (4 shorter events, 0.0 us)
Async XLA Ops:
  7.2 4.9 %copy-start = (bf16[64,64,256]{2,1,0:T(8,128)(2,1)S(1)}, bf16[64,64,256]{2,1,0:T(8,128)(2,1)}, u32[]{:S(2)}) copy-start(bf16[64,64,256]{2,1,0:T(8,128)(2,1)} %param.9) | copy-start | bytes 6291460
  7.2 58.6 %all-gather.2.cloned.1.call-start = ((), (), s32[]{:S(2)}) async-start(), calls=%async_computation.1 | async-start | bytes 2359296 | tf_op jit(solution)/shard_map/all_gather | solution.py:66
  12.1 1.6 copy-start.1
  13.6 145.6 %reduce-scatter.2.cloned.1.call-start = ((), (), s32[]{:S(2)}) async-start(), calls=%async_computation.2 | async-start | bytes 2359296 | tf_op jit(solution)/shard_map/reduce_scatter | solution.py:71
Sparse Core Ops, SparseCore 0:
  13.8 51.9 all-gather.1
  92.5 66.7 reduce-scatter.1
where the time goes:
time: 166 us
  waiting for transfers between devices  118 us (71%)
  matrix products  20 us (12%)
  between operations  14.1 us (8%)
  blocking collectives  10.3 us (6%)
  local copies, waits for them, and re-layouts  2.29 us (1%)
    reduce_scatter x1, waiting for transfers between devices, on_device(): lax.psum_scatter(lax.dot_general(picker, adapter_delta, (((0,), (0,)), ((...  66.9 us
    all_gather x1, waiting for transfers between devices, on_device(): lax.all_gather(decode_attention, 'req', axis=0, tiled=True)  50.9 us
    psum x1, blocking collectives, apply_adapter(): shrink = lax.psum(partial_shrink, 'tp').astype(jnp.bfloat16)  10.3 us
    dot_general x1, matrix products, apply_adapter(): jnp.einsum('pv,hvo->pho', incoming_slots, down_weight, preferred_element_...  8.5 us
    dot_general x1, matrix products, on_device(): lax.dot_general(picker, adapter_delta, (((0,), (0,)), ((), ())), preferre...  7.03 us
  transfers between devices with their start and end apart: 2, of which 2 were waited for; matrix products, arithmetic and copies ran while one was open for 1% of the time, Pallas kernels for 0%

commit v1 on v0

v1 whole, which is shorter than its diff:
```python
import functools

import jax
import jax.numpy as jnp
from jax import lax
from jax.experimental import pallas as pl
from jax.experimental.pallas import tpu as pltpu
from jax.sharding import PartitionSpec as P

HEAD_DIM = 128
CAP = 8
CTX = 64
GROUP = 8
RANK = 64
SUB = 8
BLOCK = 16
MESH = pl.DeviceIdType.MESH
F32 = jnp.float32
BF16 = jnp.bfloat16
NT = (((1,), (1,)), ((), ()))
NN = (((1,), (0,)), ((), ()))
TN = (((0,), (0,)), ((), ()))


def dot(a, b, dims=NN):
    return lax.dot_general(a, b, dims, preferred_element_type=F32)


def swap_halves(x):
    return jnp.concatenate([x[:, RANK:], x[:, :RANK]], axis=1)


def ranks_in_block(onehot):
    rows = onehot.shape[1]
    before = lax.broadcasted_iota(jnp.int32, (rows, rows), 0)
    after = lax.broadcasted_iota(jnp.int32, (rows, rows), 1)
    earlier = jnp.where(before < after, 1.0, 0.0).astype(BF16)
    return dot(onehot.astype(BF16), earlier)


def to_blocks(x, n_req):
    half = x.shape[1] // 2
    out = []
    for o in range(n_req):
        tile = x[o * CAP : (o + 1) * CAP]
        out.append(jnp.concatenate([tile[:, :half], tile[:, half:]], axis=0).astype(BF16))
    return out


def from_blocks(blocks):
    n_req, _, half = blocks.shape
    wide = blocks.astype(F32)
    low = wide[:, :CAP].reshape(n_req * CAP, half)
    high = wide[:, CAP:].reshape(n_req * CAP, half)
    return jnp.concatenate([low, high], axis=1).astype(BF16)


def kernel(
    n_req, n_tp, adapters,
    q_hbm, k_hbm, v_hbm, lengths_ref, index_ref, down_hbm, up_hbm,
    attn_ref, out_ref,
    q, k, v, down, up, send1, recv1, send2, recv2, partial, peers, len_ref,
    load_sem, kv_sem, s1, r1, s2, r2, s3, r3,
):
    rows, width = q.shape
    slots = n_req * CAP
    kv_local = k.shape[1] // HEAD_DIM
    span = GROUP * HEAD_DIM
    parts = kv_local
    me = lax.axis_index("req")
    my_tp = lax.axis_index("tp")

    q_copy = pltpu.make_async_copy(q_hbm, q, load_sem.at[0])
    q_copy.start()
    n_blocks = rows // BLOCK
    kv_rows = BLOCK * CTX

    def kv_copies(b):
        at = pl.ds(pl.multiple_of(b * kv_rows, kv_rows), kv_rows)
        return (
            pltpu.make_async_copy(k_hbm.at[at], k.at[at], kv_sem.at[0, b]),
            pltpu.make_async_copy(v_hbm.at[at], v.at[at], kv_sem.at[1, b]),
        )

    for b in range(n_blocks):
        for copy in kv_copies(b):
            copy.start()
    down_copy = pltpu.make_async_copy(down_hbm, down, load_sem.at[1])
    down_copy.start()
    up_copy = pltpu.make_async_copy(up_hbm, up, load_sem.at[2])
    up_copy.start()

    barrier = pltpu.get_barrier_semaphore()
    req_to = [lax.rem(me + d, n_req) for d in range(n_req)]
    tp_to = [lax.rem(my_tp + d, n_tp) for d in range(n_tp)]
    for d in range(1, n_req):
        pl.semaphore_signal(barrier, inc=1, device_id=(req_to[d], my_tp), device_id_type=MESH)
    for d in range(1, n_tp):
        pl.semaphore_signal(barrier, inc=1, device_id=(me, tp_to[d]), device_id_type=MESH)

    index = index_ref[...]
    spread_index = jnp.broadcast_to(index[:, None, :], (n_req, CAP, rows)).reshape(slots, rows)
    slot_iota = lax.broadcasted_iota(jnp.int32, (slots, rows), 0)
    slot_rank = (slot_iota % CAP).astype(F32)
    owner_of_slot = slot_iota // CAP
    mine = jnp.broadcast_to(index_ref[pl.ds(me, 1), :], (slots, rows))
    to_owner = jnp.where(mine // adapters == owner_of_slot, 1.0, 0.0)
    pack = jnp.where(ranks_in_block(to_owner) == slot_rank, to_owner, 0.0).astype(BF16)
    to_me = jnp.where(spread_index // adapters == me, 1.0, 0.0)
    taken = jnp.where(ranks_in_block(to_me) == slot_rank, to_me, 0.0)
    local = (spread_index % adapters + 1).astype(F32)
    adapter = jnp.sum(taken * local, axis=1, keepdims=True).astype(jnp.int32) - 1

    row_r = lax.broadcasted_iota(jnp.int32, (rows, rows), 0)
    row_c = lax.broadcasted_iota(jnp.int32, (rows, rows), 1)
    len_row = jnp.broadcast_to(lengths_ref[...].astype(F32), (rows, rows))
    len_col = jnp.sum(jnp.where(row_r == row_c, len_row, 0.0), axis=1, keepdims=True)
    len_ref[...] = jnp.broadcast_to(len_col.astype(jnp.int32), len_ref.shape)

    q_copy.wait()
    keys = SUB * CTX
    place = lax.broadcasted_iota(jnp.int32, (SUB, keys), 1) - CTX * lax.broadcasted_iota(
        jnp.int32, (SUB, keys), 0
    )

    def exchange(m, d, src, dst, ssem, rsem):
        return pltpu.make_async_remote_copy(
            src_ref=src.at[m, req_to[d]],
            dst_ref=dst.at[m, me],
            send_sem=ssem.at[m, d],
            recv_sem=rsem.at[m, d],
            device_id=(req_to[d], my_tp),
            device_id_type=MESH,
        )

    for m in range(kv_local):
        cols = slice(m * HEAD_DIM, (m + 1) * HEAD_DIM)

        def attend(b, carry):
            if m == 0:
                for copy in kv_copies(b):
                    copy.wait()
            at = pl.ds(pl.multiple_of(b * BLOCK, BLOCK), BLOCK)
            q_block = q[at, m * span : (m + 1) * span].astype(F32)
            mixed = []
            for s in range(BLOCK // SUB):
                kv_at = pl.ds(pl.multiple_of(b * kv_rows + s * keys, keys), keys)
                q_rows = q_block[s * SUB : (s + 1) * SUB]
                q_heads = jnp.concatenate(
                    [q_rows[:, h * HEAD_DIM : (h + 1) * HEAD_DIM] for h in range(GROUP)], axis=0
                ).astype(BF16)
                scores = dot(q_heads, k[kv_at, cols], NT) * HEAD_DIM ** (-0.5)
                length = len_ref[pl.ds(pl.multiple_of(b * BLOCK + s * SUB, SUB), SUB), 0:1]
                live = jnp.logical_and(place >= 0, place < length)
                live = jnp.concatenate([live] * GROUP, axis=0)
                scores = jnp.where(live, scores, -jnp.inf)
                highest = jnp.max(scores, axis=1, keepdims=True)
                expo = jnp.exp(scores - highest)
                weights = (expo * (1.0 / jnp.sum(expo, axis=1, keepdims=True))).astype(BF16)
                mixed.append(dot(weights, v[kv_at, cols]))
            for h in range(GROUP):
                tile = jnp.concatenate([x[h * SUB : (h + 1) * SUB] for x in mixed], axis=0)
                first = m * span + h * HEAD_DIM
                attn_ref[at, first : first + HEAD_DIM] = tile.astype(BF16)
            return carry

        lax.fori_loop(0, n_blocks, attend, 0)
        packed = dot(pack, attn_ref[:, m * span : (m + 1) * span])
        for o, block in enumerate(to_blocks(packed, n_req)):
            send1[m, o] = block
        recv1[m, me] = send1[m, me]
        if m == 0:
            pl.semaphore_wait(barrier, n_req - 1 + n_tp - 1)
        for d in range(1, n_req):
            exchange(m, d, send1, recv1, s1, r1).start()

    tile_w = 4 * RANK
    lane = lax.broadcasted_iota(jnp.int32, (slots, 2 * RANK), 1)
    odd = jnp.where(lane >= RANK, 1, 0)
    pair_of_lane = adapter - odd

    down_copy.wait()
    total = jnp.zeros((slots, 2 * RANK), F32)
    for m in range(parts):
        for d in range(1, n_req):
            exchange(m, d, send1, recv1, s1, r1).wait_recv()
        x = from_blocks(recv1[m])

        def shrink_tile(c, acc):
            at = pl.ds(pl.multiple_of(c * tile_w, tile_w), tile_w)
            both = dot(x, down[at, m * span : (m + 1) * span], NT)
            for i in range(2):
                keep = pair_of_lane == 4 * c + 2 * i
                acc = acc + jnp.where(keep, both[:, i * 2 * RANK : (i + 1) * 2 * RANK], 0.0)
            return acc

        total = lax.fori_loop(0, adapters * RANK // tile_w, shrink_tile, total)

    folded = total + swap_halves(total)
    low = lax.broadcasted_iota(jnp.int32, (slots // 2, 2 * RANK), 1) < RANK
    partial[...] = jnp.where(low, folded[: slots // 2], folded[slots // 2 :])

    def share(d):
        return pltpu.make_async_remote_copy(
            src_ref=partial,
            dst_ref=peers.at[d],
            send_sem=s3.at[d],
            recv_sem=r3.at[d],
            device_id=(me, tp_to[d]),
            device_id_type=MESH,
        )

    for d in range(1, n_tp):
        share(d).start()
    shrink = partial[...]
    for d in range(1, n_tp):
        share(d).wait_recv()
        shrink = shrink + peers[d]
    swapped = swap_halves(shrink)
    shrink = jnp.concatenate([jnp.where(low, shrink, swapped), jnp.where(low, swapped, shrink)], axis=0)
    spread = jnp.concatenate(
        [jnp.where(pair_of_lane == 2 * j, shrink, 0.0).astype(BF16) for j in range(adapters // 2)],
        axis=1,
    )

    up_copy.wait()
    for m in range(parts):
        term = dot(spread, up[:, m * span : (m + 1) * span])
        for o, block in enumerate(to_blocks(term, n_req)):
            send2[m, o] = block
        recv2[m, me] = send2[m, me]
        for d in range(1, n_req):
            exchange(m, d, send2, recv2, s2, r2).start()
    for m in range(parts):
        for d in range(1, n_req):
            exchange(m, d, send2, recv2, s2, r2).wait_recv()
        y = from_blocks(recv2[m])
        out_ref[:, m * span : (m + 1) * span] = dot(pack, y, TN).astype(BF16)

    for m in range(parts):
        for d in range(1, n_req):
            exchange(m, d, send1, recv1, s1, r1).wait_send()
            exchange(m, d, send2, recv2, s2, r2).wait_send()
    for d in range(1, n_tp):
        share(d).wait_send()


def on_device(n_req, n_tp, queries, key_cache, value_cache, lengths, index, down_weight, up_weight):
    rows, width = queries.shape
    kv_width = key_cache.shape[2]
    kv_local = kv_width // HEAD_DIM
    adapters = down_weight.shape[0]
    slots = n_req * CAP
    half = GROUP * HEAD_DIM // 2
    out = jax.ShapeDtypeStruct((rows, width), BF16)
    hbm = pl.BlockSpec(memory_space=pl.ANY)
    vmem = pl.BlockSpec(memory_space=pltpu.VMEM)
    blocks = pltpu.VMEM((kv_local, n_req, 2 * CAP, half), BF16)
    dma = pltpu.SemaphoreType.DMA
    return pl.pallas_call(
        functools.partial(kernel, n_req, n_tp, adapters),
        out_shape=(out, out),
        in_specs=[hbm, hbm, hbm, vmem, vmem, hbm, hbm],
        out_specs=(vmem, vmem),
        scratch_shapes=[
            pltpu.VMEM((rows, width), BF16),
            pltpu.VMEM((rows * CTX, kv_width), BF16),
            pltpu.VMEM((rows * CTX, kv_width), BF16),
            pltpu.VMEM((adapters * RANK, width), BF16),
            pltpu.VMEM((adapters * RANK, width), BF16),
            blocks, blocks, blocks, blocks,
            pltpu.VMEM((slots // 2, 2 * RANK), F32),
            pltpu.VMEM((n_tp, slots // 2, 2 * RANK), F32),
            pltpu.VMEM((rows, HEAD_DIM), jnp.int32),
            dma((3,)),
            dma((2, rows // BLOCK)),
            dma((kv_local, n_req)), dma((kv_local, n_req)),
            dma((kv_local, n_req)), dma((kv_local, n_req)),
            dma((n_tp,)), dma((n_tp,)),
        ],
        compiler_params=pltpu.CompilerParams(
            collective_id=0, has_side_effects=True, vmem_limit_bytes=48 * 2**20
        ),
        cost_estimate=pl.CostEstimate(
            flops=4 * slots * adapters * RANK * width, bytes_accessed=22 * 2**20, transcendentals=0
        ),
    )(
        queries,
        key_cache.reshape(rows * CTX, kv_width),
        value_cache.reshape(rows * CTX, kv_width),
        lengths.reshape(1, rows),
        index.reshape(n_req, rows),
        jnp.swapaxes(down_weight, 1, 2).reshape(adapters * RANK, width),
        up_weight.reshape(adapters * RANK, width),
    )


def solution(mesh):
    in_specs = (
        P("req", "tp"),
        P("req", None, "tp"),
        P("req", None, "tp"),
        P("req"),
        P(),
        P("req", "tp", None),
        P("req", None, "tp"),
    )
    out_specs = (P("req", "tp"), P("req", "tp"))
    return jax.shard_map(
        functools.partial(on_device, mesh.shape["req"], mesh.shape["tp"]),
        mesh=mesh, in_specs=in_specs, out_specs=out_specs, check_vma=False,
    )
```

time: 166 us -> 38.2 us (0.23)
  waiting for transfers between devices: 118 us -> 0 us
  Pallas kernels: 0 us -> 30.4 us
  matrix products: 20 us -> 0 us
  between operations: 14.1 us -> 0.64 us
  blocking collectives: 10.3 us -> 0 us
  local copies, waits for them, and re-layouts: 2.29 us -> 6.95 us
    reduce_scatter x1 -> x0, waiting for transfers between devices: 66.9 us -> none  [on_device(): lax.psum_scatter(lax.dot_general(picker, adapter_delta, (((0,), (0,)), ((...]
    all_gather x1 -> x0, waiting for transfers between devices: 50.9 us -> none  [on_device(): lax.all_gather(decode_attention, 'req', axis=0, tiled=True)]
    pallas_call x0 -> x1, Pallas kernels: none -> 30.4 us  [on_device(): pl.pallas_call(functools.partial(kernel, n_req, n_tp, adapters), out_shap...]
    dot_general x5 -> x0, matrix products: 17 us -> none  [the longest x1 8.5 us: apply_adapter(): jnp.einsum('pv,hvo->pho', incoming_slots, down_weight, preferred_element_...]
    psum x1 -> x0, blocking collectives: 10.3 us -> none  [apply_adapter(): shrink = lax.psum(partial_shrink, 'tp').astype(jnp.bfloat16)]
    unnamed x6 -> x10, local copies, waits for them, and re-layouts: 1.92 us -> 6.19 us
    sub x1 -> x0, matrix products: 2.99 us -> none  [attend(): expo = jnp.exp(scores - highest)]
  transfers between devices with their start and end apart: 2 -> 0, of which waited for: 2 -> 0; matrix products, arithmetic and copies ran while one was open for 1% -> 0% of each run, Pallas kernels for 0% -> 0%
where the time goes in v1:
time: 38.2 us; the launch traced here: 37.9 us
  Pallas kernels  30.4 us (80%)
  local copies, waits for them, and re-layouts  6.95 us (18%)
  between operations  0.64 us (2%)
    pallas_call x1, Pallas kernels, on_device(): pl.pallas_call(functools.partial(kernel, n_req, n_tp, adapters), out_shap...  30.4 us
    unnamed x10, local copies, waits for them, and re-layouts  6.19 us

profile of v1, /device:TPU:0, one launch (start us, length us, event | category | flops | bytes accessed | tf_op | source)
XLA Modules:
  0.0 37.9 jit_solution(4197516878566461624)
XLA Ops:
  0.6 0.8 %reshape.25.index_ref = s32[8,64]{1,0:T(8,128)S(1)} reshape(s32[512]{0:T(512)} %param.11) | data formatting | bytes 4096 | tf_op jit(solution)/shard_map/reshape | solution.py:292
  1.4 0.0 copy-start
  1.4 1.6 %copy-done = bf16[64,64,256]{2,1,0:T(8,128)(2,1)S(1)} copy-done((bf16[64,64,256]{2,1,0:T(8,128)(2,1)S(1)}, bf16[64,64,256]{2,1,0:T(8,128)(2,1)}, u32[]{:S(2)}) %copy-start) | copy-done | bytes 2097176
  3.0 0.0 copy-start.1
  3.0 1.6 %copy-done.1 = bf16[64,64,256]{2,1,0:T(8,128)(2,1)S(1)} copy-done((bf16[64,64,256]{2,1,0:T(8,128)(2,1)S(1)}, bf16[64,64,256]{2,1,0:T(8,128)(2,1)}, u32[]{:S(2)}) %copy-start.1) | copy-done | bytes 2097176
  4.6 0.0 copy-start.2
  4.6 0.9 %copy-done.2 = bf16[64,2048]{1,0:T(8,128)(2,1)S(1)} copy-done((bf16[64,2048]{1,0:T(8,128)(2,1)S(1)}, bf16[64,2048]{1,0:T(8,128)(2,1)}, u32[]{:S(2)}) %copy-start.2) | copy-done | bytes 262168
  5.5 0.0 copy-start.3
  5.5 0.7 %copy-done.3 = s32[64]{0:T(128)S(1)} copy-done((s32[64]{0:T(128)S(1)}, s32[64]{0:T(128)}, u32[]{:S(2)}) %copy-start.3) | copy-done | bytes 280
  6.2 30.4 %shard_map.86 = (bf16[64,2048]{1,0:T(8,128)(2,1)S(1)}, bf16[64,2048]{1,0:T(8,128)(2,1)S(1)}) custom-call(bf16[64,2048]{1,0:T(8,128)(2,1)S(1)} %copy-done.2, bf16[4096,256]{1,0:T(8,128)(2,1)S(1)} %bitcast.7, bf16[4096,256]{1,0:T(8,128)(2,1)S(1)} %bitcast.8, s32[1,64]{1,0:T(1,128)S(1)} %bitcast.9, s32[8,64]{1,0:T(8,128)S(1)} %reshape.25.index_ref, ...), custom_call_target="tpu_custom_call" | custom-call | flops 1073741824 | bytes 23068672 | tf_op jit(solution)/shard_map/pallas_call | solution.py:260
  36.5 0.7 %copy.11 = bf16[64,2048]{1,0:T(8,128)(2,1)} copy(bf16[64,2048]{1,0:T(8,128)(2,1)S(1)} %get-tuple-element.4) | data formatting | bytes 524288
  37.2 0.7 %copy.12 = bf16[64,2048]{1,0:T(8,128)(2,1)} copy(bf16[64,2048]{1,0:T(8,128)(2,1)S(1)} %get-tuple-element.5) | data formatting | bytes 524288
Async XLA Ops:
  1.4 1.6 %copy-start = (bf16[64,64,256]{2,1,0:T(8,128)(2,1)S(1)}, bf16[64,64,256]{2,1,0:T(8,128)(2,1)}, u32[]{:S(2)}) copy-start(bf16[64,64,256]{2,1,0:T(8,128)(2,1)} %param.8) | copy-start | bytes 6291460
  3.0 1.6 %copy-start.1 = (bf16[64,64,256]{2,1,0:T(8,128)(2,1)S(1)}, bf16[64,64,256]{2,1,0:T(8,128)(2,1)}, u32[]{:S(2)}) copy-start(bf16[64,64,256]{2,1,0:T(8,128)(2,1)} %param.9) | copy-start | bytes 6291460
  4.6 0.9 %copy-start.2 = (bf16[64,2048]{1,0:T(8,128)(2,1)S(1)}, bf16[64,2048]{1,0:T(8,128)(2,1)}, u32[]{:S(2)}) copy-start(bf16[64,2048]{1,0:T(8,128)(2,1)} %q_hbm.1) | copy-start | bytes 786436
  5.5 0.7 %copy-start.3 = (s32[64]{0:T(128)S(1)}, s32[64]{0:T(128)}, u32[]{:S(2)}) copy-start(s32[64]{0:T(128)} %param.10) | copy-start | bytes 772

commit v2 on v1

--- a/solution.py
+++ b/solution.py
@@ -57,9 +57,9 @@
 
 def kernel(
     n_req, n_tp, adapters,
-    q_hbm, k_hbm, v_hbm, lengths_ref, index_ref, down_hbm, up_hbm,
+    q_hbm, k_hbm, v_hbm, lengths_hbm, index_hbm, down_hbm, up_hbm,
     attn_ref, out_ref,
-    q, k, v, down, up, send1, recv1, send2, recv2, partial, peers, len_ref,
+    q, k, v, down, up, send1, recv1, send2, recv2, partial, peers, len_ref, lengths_ref, index_ref,
     load_sem, kv_sem, s1, r1, s2, r2, s3, r3,
 ):
     rows, width = q.shape
@@ -70,6 +70,10 @@
     me = lax.axis_index("req")
     my_tp = lax.axis_index("tp")
 
+    index_copy = pltpu.make_async_copy(index_hbm, index_ref, load_sem.at[3])
+    index_copy.start()
+    lengths_copy = pltpu.make_async_copy(lengths_hbm, lengths_ref, load_sem.at[4])
+    lengths_copy.start()
     q_copy = pltpu.make_async_copy(q_hbm, q, load_sem.at[0])
     q_copy.start()
     n_blocks = rows // BLOCK
@@ -88,7 +92,6 @@
     down_copy = pltpu.make_async_copy(down_hbm, down, load_sem.at[1])
     down_copy.start()
     up_copy = pltpu.make_async_copy(up_hbm, up, load_sem.at[2])
-    up_copy.start()
 
     barrier = pltpu.get_barrier_semaphore()
     req_to = [lax.rem(me + d, n_req) for d in range(n_req)]
@@ -98,12 +101,22 @@
     for d in range(1, n_tp):
         pl.semaphore_signal(barrier, inc=1, device_id=(me, tp_to[d]), device_id_type=MESH)
 
-    index = index_ref[...]
-    spread_index = jnp.broadcast_to(index[:, None, :], (n_req, CAP, rows)).reshape(slots, rows)
+    index_copy.wait()
+    lengths_copy.wait()
+    spread_index = jnp.concatenate(
+        [
+            jnp.broadcast_to(index_ref[:, p * rows : (p + 1) * rows], (CAP, rows))
+            for p in range(n_req)
+        ],
+        axis=0,
+    )
     slot_iota = lax.broadcasted_iota(jnp.int32, (slots, rows), 0)
     slot_rank = (slot_iota % CAP).astype(F32)
     owner_of_slot = slot_iota // CAP
-    mine = jnp.broadcast_to(index_ref[pl.ds(me, 1), :], (slots, rows))
+    mine = spread_index[:CAP]
+    for p in range(1, n_req):
+        mine = jnp.where(me == p, spread_index[p * CAP : (p + 1) * CAP], mine)
+    mine = jnp.concatenate([mine] * n_req, axis=0)
     to_owner = jnp.where(mine // adapters == owner_of_slot, 1.0, 0.0)
     pack = jnp.where(ranks_in_block(to_owner) == slot_rank, to_owner, 0.0).astype(BF16)
     to_me = jnp.where(spread_index // adapters == me, 1.0, 0.0)
@@ -164,7 +177,7 @@
                 attn_ref[at, first : first + HEAD_DIM] = tile.astype(BF16)
             return carry
 
-        lax.fori_loop(0, n_blocks, attend, 0)
+        lax.fori_loop(0, n_blocks, attend, 0, unroll=True)
         packed = dot(pack, attn_ref[:, m * span : (m + 1) * span])
         for o, block in enumerate(to_blocks(packed, n_req)):
             send1[m, o] = block
@@ -174,6 +187,7 @@
         for d in range(1, n_req):
             exchange(m, d, send1, recv1, s1, r1).start()
 
+    up_copy.start()
     tile_w = 4 * RANK
     lane = lax.broadcasted_iota(jnp.int32, (slots, 2 * RANK), 1)
     odd = jnp.where(lane >= RANK, 1, 0)
@@ -194,7 +208,7 @@
                 acc = acc + jnp.where(keep, both[:, i * 2 * RANK : (i + 1) * 2 * RANK], 0.0)
             return acc
 
-        total = lax.fori_loop(0, adapters * RANK // tile_w, shrink_tile, total)
+        total = lax.fori_loop(0, adapters * RANK // tile_w, shrink_tile, total, unroll=True)
 
     folded = total + swap_halves(total)
     low = lax.broadcasted_iota(jnp.int32, (slots // 2, 2 * RANK), 1) < RANK
@@ -260,7 +274,7 @@
     return pl.pallas_call(
         functools.partial(kernel, n_req, n_tp, adapters),
         out_shape=(out, out),
-        in_specs=[hbm, hbm, hbm, vmem, vmem, hbm, hbm],
+        in_specs=[hbm] * 7,
         out_specs=(vmem, vmem),
         scratch_shapes=[
             pltpu.VMEM((rows, width), BF16),
@@ -272,14 +286,16 @@
             pltpu.VMEM((slots // 2, 2 * RANK), F32),
             pltpu.VMEM((n_tp, slots // 2, 2 * RANK), F32),
             pltpu.VMEM((rows, HEAD_DIM), jnp.int32),
-            dma((3,)),
+            pltpu.VMEM((1, rows), jnp.int32),
+            pltpu.VMEM((1, n_req * rows), jnp.int32),
+            dma((5,)),
             dma((2, rows // BLOCK)),
             dma((kv_local, n_req)), dma((kv_local, n_req)),
             dma((kv_local, n_req)), dma((kv_local, n_req)),
             dma((n_tp,)), dma((n_tp,)),
         ],
         compiler_params=pltpu.CompilerParams(
-            collective_id=0, has_side_effects=True, vmem_limit_bytes=48 * 2**20
+            collective_id=0, has_side_effects=True, vmem_limit_bytes=63 * 2**20
         ),
         cost_estimate=pl.CostEstimate(
             flops=4 * slots * adapters * RANK * width, bytes_accessed=22 * 2**20, transcendentals=0
@@ -289,7 +305,7 @@
         key_cache.reshape(rows * CTX, kv_width),
         value_cache.reshape(rows * CTX, kv_width),
         lengths.reshape(1, rows),
-        index.reshape(n_req, rows),
+        index.reshape(1, n_req * rows),
         jnp.swapaxes(down_weight, 1, 2).reshape(adapters * RANK, width),
         up_weight.reshape(adapters * RANK, width),
     )

time: 38.2 us -> 35.2 us (0.921)
  local copies, waits for them, and re-layouts: 6.95 us -> 3.34 us
  Pallas kernels: 30.4 us -> 31.1 us
    unnamed x10 -> x2, local copies, waits for them, and re-layouts: 6.19 us -> 3.34 us
    reshape x1 -> x0, local copies, waits for them, and re-layouts: 0.76 us -> none  [on_device(): index.reshape(n_req, rows)]
    pallas_call x1, Pallas kernels: 30.4 us -> 31.1 us  [on_device(): pl.pallas_call(functools.partial(kernel, n_req, n_tp, adapters), out_shap...]
where the time goes in v2:
time: 35.2 us; the launch traced here: 35.1 us
  Pallas kernels  31.1 us (88%)
  local copies, waits for them, and re-layouts  3.34 us (9%)
  between operations  0.64 us (2%)
    pallas_call x1, Pallas kernels, on_device(): pl.pallas_call(functools.partial(kernel, n_req, n_tp, adapters), out_shap...  31.1 us
    unnamed x2, local copies, waits for them, and re-layouts  3.34 us

profile of v2, /device:TPU:0, one launch (start us, length us, event | category | flops | bytes accessed | tf_op | source)
XLA Modules:
  0.0 35.1 jit_solution(2234066095629510278)
XLA Ops:
  0.6 31.1 %shard_map.86 = (bf16[64,2048]{1,0:T(8,128)(2,1)}, bf16[64,2048]{1,0:T(8,128)(2,1)}) custom-call(bf16[64,2048]{1,0:T(8,128)(2,1)} %q_hbm.1, bf16[4096,256]{1,0:T(8,128)(2,1)} %bitcast.10, bf16[4096,256]{1,0:T(8,128)(2,1)} %bitcast.11, s32[1,64]{1,0:T(1,128)} %bitcast.13, s32[1,512]{1,0:T(1,128)} %bitcast.12, bf16[2048,2048]{1,0:T(8,128)(2,1)} %bitcast.8, ...), custom_call_target="tpu_custom_call" | custom-call | flops 1073741824 | bytes 23068672 | tf_op jit(solution)/shard_map/pallas_call | solution.py:274
  31.7 1.7 %copy.11 = bf16[64,2048]{1,0:T(8,128)(2,1)} copy(bf16[64,2048]{1,0:T(8,128)(2,1)} %get-tuple-element.4) | data formatting | bytes 524288
  33.4 1.7 %copy.12 = bf16[64,2048]{1,0:T(8,128)(2,1)} copy(bf16[64,2048]{1,0:T(8,128)(2,1)} %get-tuple-element.5) | data formatting | bytes 524288
